TPU v7x, 32 devices: a whole 2x2x4 slice. The times are simulated.
32 devices in a mesh: groups: 2 (over y), fsdp: 4 (over z), dp: 2 (over x), pair: 2 (over core).
Axes of the slice: x: 2, y: 2, z: 4, core: 2. Of those that a mesh axis runs over, the one named last changes fastest.
Arguments:
- hidden_input: bfloat16 [4096, 8192], P(('groups', 'fsdp', 'dp', 'pair')), parts along dimension 0, may hold values from -6 to 6
- norm_gain_vector: float32 [8192], replicated, may hold values from 0.5 to 18, as said below
- value_matrix: bfloat16 [8192, 768], P('fsdp'), may hold values from -0.0625 to 0.0625
- adapter_down_map: bfloat16 [16384, 64], P(('groups', 'fsdp')), parts along dimension 0, may hold values from -0.0625 to 0.0625
- adapter_up_map: bfloat16 [128, 768], P('groups'), parts along dimension 0, may hold values from -5 to 5
- values_gradient: bfloat16 [4096, 768], P(('groups', 'fsdp', 'dp', 'pair')), parts along dimension 0, may hold values from -6 to 6
Outputs:
- grad_hidden: bfloat16 [4096, 8192], P(('groups', 'fsdp', 'dp', 'pair')), parts along dimension 0
- grad_down: float32 [16384, 64], P(('groups', 'fsdp')), parts along dimension 0
- grad_up: float32 [128, 768], P('groups'), parts along dimension 0
There are 2 independent parts, one for each index of `groups`. A program takes and returns all parts, laid end to end along the dimension named above; an argument that names none is the same for every part. Nothing has to cross between parts.
Inputs may be any that keep to these rules, and one draw needn't show every extreme that they name: `norm_gain_vector`: positive gains.
All inputs are finite; a program needn't handle non-finite values.
Results may differ from a plain program's by a relative error of at most 0.0085.
Values may be sent and summed in bfloat16 or wider, within the bound.
A program may use at most 64 MiB of HBM per device.

v0:
```python
import math
import jax
import jax.numpy as jnp
from jax import lax
from jax.sharding import PartitionSpec as P

MODEL_WIDTH = 8192
ADAPTER_RANK = 64
norm_eps = 1e-05
adapter_scale = 2.0


def contract_last(left, right):
    return lax.dot_general(
        left, right, (((1,), (1,)), ((), ())), preferred_element_type=jnp.float32
    )


def contract_leading(left, right):
    return lax.dot_general(
        left, right, (((0,), (0,)), ((), ())), preferred_element_type=jnp.float32
    )


def local(
    hidden_input, norm_gain_vector, value_matrix, adapter_down_map, adapter_up_map, values_gradient
):
    width = hidden_input.shape[1]
    stream = hidden_input.astype(jnp.float32)
    inv_rms = lax.rsqrt(jnp.mean(stream * stream, axis=1, keepdims=True) + norm_eps)
    normalized_input = (stream * inv_rms * norm_gain_vector).astype(jnp.bfloat16)
    upward_product = (
        adapter_scale
        * jnp.dot(values_gradient, adapter_up_map.T, preferred_element_type=jnp.float32)
    ).astype(jnp.bfloat16)
    every_values, every_upward = (
        lax.all_gather(values_gradient, "fsdp", axis=0, tiled=True),
        lax.all_gather(upward_product, "fsdp", axis=0, tiled=True),
    )
    columns = contract_last(every_values, value_matrix) + contract_last(
        every_upward, adapter_down_map
    )
    gradient_normalized = lax.all_to_all(
        columns.astype(jnp.bfloat16), "fsdp", split_axis=0, concat_axis=1, tiled=True
    )
    window = normalized_input
    latent_f = jnp.dot(
        window,
        lax.all_gather(adapter_down_map, "fsdp", axis=0, tiled=True),
        preferred_element_type=jnp.float32,
    )
    scaled = gradient_normalized.astype(jnp.float32) * norm_gain_vector
    grad_stream = inv_rms * scaled - stream * (inv_rms**3 / width) * jnp.sum(
        scaled * stream, axis=1, keepdims=True
    )
    latent_code = latent_f.astype(jnp.bfloat16)
    window = normalized_input
    down_shard = lax.psum_scatter(
        contract_leading(window, upward_product), "fsdp", scatter_dimension=0, tiled=True
    )
    up_portion = adapter_scale * contract_leading(latent_code, values_gradient)
    down_shard = lax.psum(down_shard, ("dp", "pair"))
    up_full = lax.psum(up_portion, ("fsdp", "dp", "pair"))
    total = lax.psum(jnp.sum(down_shard * down_shard), "fsdp") + jnp.sum(up_full * up_full)
    factor = jnp.minimum(1.0, 0.5 * math.sqrt(MODEL_WIDTH * ADAPTER_RANK) / jnp.sqrt(total))
    return (grad_stream.astype(jnp.bfloat16), factor * down_shard, factor * up_full)


def solution(mesh):
    return jax.shard_map(
        local,
        mesh=mesh,
        in_specs=(
            P(("groups", "fsdp", "dp", "pair"), None),
            P(),
            P("fsdp", None),
            P(("groups", "fsdp"), None),
            P("groups", None),
            P(("groups", "fsdp", "dp", "pair"), None),
        ),
        out_specs=(
            P(("groups", "fsdp", "dp", "pair"), None),
            P(("groups", "fsdp"), None),
            P("groups", None),
        ),
        check_vma=False,
    )
```

profile of v0, /device:TPU:0, one launch (start us, length us, event | category | flops | bytes accessed | tf_op | source)
XLA Modules:
  0.0 322.7 jit_solution(588120099054937987)
XLA Ops:
  7.2 0.0 copy-start
  7.2 0.0 reduce-scatter.2.cloned.1.call-start
  7.2 21.6 %all_gather.9 = bf16[512,768]{1,0:T(8,128)(2,1)S(1)} all-gather(bf16[128,768]{1,0:T(8,128)(2,1)} %param.11), channel_id=1, replica_groups=mesh['groups'=2,'fsdp'=4,'dp'=2,'pair'=2] {'fsdp'}, dimensions={0}, use_global_device_ids=true | all-gather | bytes 983040 | tf_op jit(solution)/shard_map/all_gather | solution.py:37
  28.9 1.2 fusion.7
  30.1 12.0 %all_gather.10 = bf16[512,64]{0,1:T(8,128)(2,1)S(1)} all-gather(bf16[128,64]{0,1:T(8,128)(2,1)S(1)} %fusion.7), channel_id=1, replica_groups=mesh['groups'=2,'fsdp'=4,'dp'=2,'pair'=2] {'fsdp'}, dimensions={0}, use_global_device_ids=true | all-gather | bytes 81920 | tf_op jit(solution)/shard_map/all_gather | solution.py:38
  42.0 0.0 copy-done
  42.1 0.0 copy-start.3
  42.1 1.8 fusion.13
  43.9 0.0 copy-done.3
  43.9 0.7 add_convert_fusion
  44.6 46.4 %all_to_all.13 = bf16[4,128,2048]{2,1,0:T(8,128)(2,1)S(1)} all-to-all(bf16[4,128,2048]{2,1,0:T(8,128)(2,1)S(1)} %bitcast.16), channel_id=1, replica_groups=mesh['groups'=2,'fsdp'=4,'dp'=2,'pair'=2] {'fsdp'}, dimensions={0} | all-to-all | bytes 4194304 | tf_op jit(solution)/shard_map/all_to_all | solution.py:43
  91.1 0.5 convert_bitcast_fusion
  91.6 0.0 copy-start.2
  91.6 0.0 copy-start.5
  91.6 0.5 copy.10
  92.1 0.0 copy-start.1
  92.1 1.9 copy-done.1
  94.0 0.0 copy-done.2
  94.0 0.0 copy-done.5
  94.0 1.2 fusion
  95.2 0.0 copy-start.4
  95.2 2.2 fusion.10
  97.4 0.0 reduce-scatter.2.cloned.1.call-update
  97.4 0.0 all-gather.2.cloned.1.call-start
  97.5 0.7 all-gather.2.cloned.1.call-update
  98.2 0.0 all-reduce.3.cloned.1.call-start
  98.2 42.3 %reduce-scatter.2.cloned.1.call-done = f32[2048,64]{0,1:T(8,128)} async-done(((f32[8192,64]{0,1:T(8,128)}), f32[2048,64]{0,1:T(8,128)}) %reduce-scatter.2.cloned.1.call-update) | async-done | bytes 524304 | tf_op jit(solution)/shard_map/reduce_scatter | solution.py:58
  140.5 0.0 all-reduce.3.cloned.1.call-update
  140.6 0.0 all-reduce.5.cloned.1.call-start
  140.6 28.9 %all-gather.2.cloned.1.call-done = bf16[8192,64]{0,1:T(8,128)(2,1)} async-done(((bf16[2048,64]{0,1:T(8,128)(2,1)}), bf16[8192,64]{0,1:T(8,128)(2,1)}) %all-gather.2.cloned.1.call-update) | async-done | bytes 1048592 | tf_op jit(solution)/shard_map/all_gather | solution.py:49
  169.5 0.0 copy-done.4
  169.5 3.5 %convolution_multiply_fusion = f32[64,768]{1,0:T(8,128)} fusion(bf16[128,768]{1,0:T(8,128)(2,1)S(1)} %copy-done.4, bf16[8192,64]{0,1:T(8,128)(2,1)} %all-gather.2.cloned.1.call-done, bf16[128,8192]{1,0:T(8,128)(2,1)} %param.6, f32[8192]{0:T(1024)S(1)} %copy-done.5, f32[128]{0:T(128)S(1)} %get-tuple-element.5), kind=kOutput, calls=%fused_computation.13 | convolution fusion | flops 151052288 | bytes 3572224 | tf_op jit(solution)/shard_map/dot_general | solution.py:20
  173.0 0.0 all-reduce.5.cloned.1.call-update
  173.1 5.3 %fusion.3 = bf16[128,8192]{1,0:T(8,128)(2,1)} fusion(bf16[128,8192]{1,0:T(8,128)(2,1)} %param.6, f32[128,8192]{1,0:T(8,128)} %bitcast.15, f32[128]{0:T(128)S(1)} %get-tuple-element.4, f32[128]{0:T(128)S(1)} %get-tuple-element.6, f32[8192]{0:T(1024)S(1)} %copy-done.5, f32[128]{0:T(128)S(1)} %get-tuple-element.5), kind=kLoop, calls=%fused_computation.7 | loop fusion | flops 7340032 | bytes 8422912 | tf_op jit(solution)/shard_map/convert_element_type | solution.py:66
  178.4 26.3 %all-reduce.3.cloned.1.call-done = f32[2048,64]{0,1:T(8,128)} async-done(((f32[2048,64]{0,1:T(8,128)}), f32[2048,64]{0,1:T(8,128)}) %all-reduce.3.cloned.1.call-update) | async-done | bytes 524304 | tf_op jit(solution)/shard_map/psum | solution.py:62
  204.7 1.8 multiply_reduce_fusion
  206.5 92.0 %all-reduce.5.cloned.1.call-done = f32[64,768]{1,0:T(8,128)} async-done(((f32[64,768]{1,0:T(8,128)}), f32[64,768]{1,0:T(8,128)}) %all-reduce.5.cloned.1.call-update) | async-done | bytes 196624 | tf_op jit(solution)/shard_map/psum | solution.py:63
  298.5 1.6 multiply_reduce_fusion.1
  300.1 11.2 %psum.22 = f32[]{:T(128)} all-reduce(f32[]{:T(128)} %multiply_reduce_fusion), channel_id=1, replica_groups=mesh['groups'=2,'fsdp'=4,'dp'=2,'pair'=2] {'fsdp'}, use_global_device_ids=true, to_apply=%region_5.0 | all-reduce | flops 1 | bytes 8 | tf_op jit(solution)/shard_map/psum | solution.py:64
  312.7 1.9 broadcast_multiply_fusion
  314.6 1.6 broadcast_multiply_fusion.1
  (1 shorter events, 0.0 us)
Async XLA Ops:
  7.2 34.9 %copy-start = (bf16[2048,768]{1,0:T(8,128)(2,1)S(1)}, bf16[2048,768]{1,0:T(8,128)(2,1)}, u32[]{:S(2)}) copy-start(bf16[2048,768]{1,0:T(8,128)(2,1)} %param.8) | copy-start | bytes 9437188
  7.2 133.4 %reduce-scatter.2.cloned.1.call-start = ((), (), s32[]{:S(2)}) async-start(), calls=%async_computation.2 | async-start | bytes 2621440 | tf_op jit(solution)/shard_map/reduce_scatter | solution.py:58
  42.1 1.8 copy-start.3
  91.6 2.5 copy-start.2
  91.6 2.4 copy-start.5
  92.1 1.9 copy-start.1
  95.2 74.3 %copy-start.4 = (bf16[128,768]{1,0:T(8,128)(2,1)S(1)}, bf16[128,768]{1,0:T(8,128)(2,1)}, u32[]{:S(2)}) copy-start(bf16[128,768]{1,0:T(8,128)(2,1)} %param.11) | copy-start | bytes 589828
  97.4 72.1 %all-gather.2.cloned.1.call-start = ((), (), s32[]{:S(2)}) async-start(), calls=%async_computation.4 | async-start | bytes 1310720 | tf_op jit(solution)/shard_map/all_gather | solution.py:49
  98.2 106.5 %all-reduce.3.cloned.1.call-start = ((), (), s32[]{:S(2)}) async-start(), calls=%async_computation.3 | async-start | bytes 1048576 | tf_op jit(solution)/shard_map/psum | solution.py:62
  140.6 157.9 %all-reduce.5.cloned.1.call-start = ((), (), s32[]{:S(2)}) async-start(), calls=%async_computation.5 | async-start | bytes 393216 | tf_op jit(solution)/shard_map/psum | solution.py:63
Sparse Core Ops, SparseCore 0:
  97.6 42.9 reduce-scatter.1
  142.2 27.2 all-gather.1
  172.0 32.6 all-reduce.2
  208.9 89.5 all-reduce.4
where the time goes:
time: 323 us
  waiting for transfers between devices  190 us (59%)
  blocking collectives  91.3 us (28%)
  between operations  15.2 us (5%)
  other arithmetic  13.9 us (4%)
  matrix products  9.43 us (3%)
    psum x1, waiting for transfers between devices, local(): up_full = lax.psum(up_portion, ('fsdp', 'dp', 'pair'))  92 us
    all_to_all x1, blocking collectives, local(): lax.all_to_all(columns.astype(jnp.bfloat16), 'fsdp', split_axis=0, concat...  46.4 us
    reduce_scatter x1, waiting for transfers between devices, local(): lax.psum_scatter(contract_leading(window, upward_product), 'fsdp', scatte...  42.3 us
    all_gather x1, waiting for transfers between devices, local(): lax.all_gather(adapter_down_map, 'fsdp', axis=0, tiled=True)  28.9 us
    psum x1, waiting for transfers between devices, local(): down_shard = lax.psum(down_shard, ('dp', 'pair'))  26.3 us
    all_gather x1, blocking collectives, local(): lax.all_gather(values_gradient, 'fsdp', axis=0, tiled=True)  21.6 us
    all_gather x1, blocking collectives, local(): lax.all_gather(upward_product, 'fsdp', axis=0, tiled=True)  12 us
    psum x1, blocking collectives, local(): lax.psum(jnp.sum(down_shard * down_shard), 'fsdp')  11.2 us
  transfers between devices with their start and end apart: 4, of which 4 were waited for; matrix products, arithmetic and copies ran while one was open for 3% of the time, Pallas kernels for 0%

commit v1 on v0

--- a/solution.py
+++ b/solution.py
@@ -60,7 +60,7 @@
     )
     up_portion = adapter_scale * contract_leading(latent_code, values_gradient)
     down_shard = lax.psum(down_shard, ("dp", "pair"))
-    up_full = lax.psum(up_portion, ("fsdp", "dp", "pair"))
+    up_full = lax.psum(lax.psum(up_portion, ("dp", "pair")), "fsdp")
     total = lax.psum(jnp.sum(down_shard * down_shard), "fsdp") + jnp.sum(up_full * up_full)
     factor = jnp.minimum(1.0, 0.5 * math.sqrt(MODEL_WIDTH * ADAPTER_RANK) / jnp.sqrt(total))
     return (grad_stream.astype(jnp.bfloat16), factor * down_shard, factor * up_full)

time: 323 us -> 249 us (0.77)
  blocking collectives: 91.3 us -> 46 us
  waiting for transfers between devices: 190 us -> 154 us
  starting transfers between devices: 0.16 us -> 4.6 us
    psum x1, waiting for transfers between devices: 92 us -> 17.6 us  [local(): up_full = lax.psum(lax.psum(up_portion, ('dp', 'pair')), 'fsdp')]
    all_to_all x0 -> x1, waiting for transfers between devices: none -> 59.7 us  [local(): lax.all_to_all(columns.astype(jnp.bfloat16), 'fsdp', split_axis=0, concat...]
    all_to_all x1 -> x0, blocking collectives: 46.4 us -> none  [local(): lax.all_to_all(columns.astype(jnp.bfloat16), 'fsdp', split_axis=0, concat...]
    all_gather x1, waiting for transfers between devices: 28.9 us -> 0.02 us  [local(): lax.all_gather(adapter_down_map, 'fsdp', axis=0, tiled=True)]
    psum x1, waiting for transfers between devices: 26.3 us -> 36.9 us  [local(): down_shard = lax.psum(down_shard, ('dp', 'pair'))]
    all_to_all x0 -> x1, starting transfers between devices: none -> 4.44 us  [local(): lax.all_to_all(columns.astype(jnp.bfloat16), 'fsdp', split_axis=0, concat...]
  transfers between devices with their start and end apart: 4 -> 5, of which waited for: 4 -> 4; matrix products, arithmetic and copies ran while one was open for 3% -> 6% of each run, Pallas kernels for 0% -> 0%
where the time goes in v1:
time: 249 us
  waiting for transfers between devices  154 us (62%)
  blocking collectives  46 us (18%)
  other arithmetic  15.5 us (6%)
  between operations  15.2 us (6%)
  matrix products  10.8 us (4%)
  starting transfers between devices  4.6 us (2%)
    all_to_all x1, waiting for transfers between devices, local(): lax.all_to_all(columns.astype(jnp.bfloat16), 'fsdp', split_axis=0, concat...  59.7 us
    reduce_scatter x1, waiting for transfers between devices, local(): lax.psum_scatter(contract_leading(window, upward_product), 'fsdp', scatte...  39.5 us
    psum x1, waiting for transfers between devices, local(): down_shard = lax.psum(down_shard, ('dp', 'pair'))  36.9 us
    all_gather x1, blocking collectives, local(): lax.all_gather(values_gradient, 'fsdp', axis=0, tiled=True)  21.6 us
    psum x1, waiting for transfers between devices, local(): up_full = lax.psum(lax.psum(up_portion, ('dp', 'pair')), 'fsdp')  17.6 us
    psum x1, blocking collectives, local(): lax.psum(jnp.sum(down_shard * down_shard), 'fsdp')  12.4 us
    all_gather x1, blocking collectives, local(): lax.all_gather(upward_product, 'fsdp', axis=0, tiled=True)  12 us
    dot_general x2, matrix products, contract_leading(): lax.dot_general(left, right, (((0,), (0,)), ((), ())), preferred_element_...  5.71 us
  transfers between devices with their start and end apart: 5, of which 4 were waited for; matrix products, arithmetic and copies ran while one was open for 6% of the time, Pallas kernels for 0%

profile of v1, /device:TPU:0, one launch (start us, length us, event | category | flops | bytes accessed | tf_op | source)
XLA Modules:
  0.0 248.9 jit_solution(16437206864968096997)
XLA Ops:
  7.2 0.0 copy-start
  7.2 21.6 %all_gather.9 = bf16[512,768]{1,0:T(8,128)(2,1)S(1)} all-gather(bf16[128,768]{1,0:T(8,128)(2,1)} %param.11), channel_id=1, replica_groups=mesh['groups'=2,'fsdp'=4,'dp'=2,'pair'=2] {'fsdp'}, dimensions={0}, use_global_device_ids=true | all-gather | bytes 983040 | tf_op jit(solution)/shard_map/all_gather | solution.py:37
  28.8 1.2 fusion.7
  30.0 12.0 %all_gather.10 = bf16[512,64]{0,1:T(8,128)(2,1)S(1)} all-gather(bf16[128,64]{0,1:T(8,128)(2,1)S(1)} %fusion.7), channel_id=1, replica_groups=mesh['groups'=2,'fsdp'=4,'dp'=2,'pair'=2] {'fsdp'}, dimensions={0}, use_global_device_ids=true | all-gather | bytes 81920 | tf_op jit(solution)/shard_map/all_gather | solution.py:38
  42.0 0.0 copy-done
  42.0 0.0 copy-start.3
  42.0 1.8 fusion.13
  43.8 0.0 copy-done.3
  43.8 2.1 add_convert_fusion
  45.9 4.4 %all-to-all-start = ((bf16[4,128,2048]{2,1,0:T(8,128)(2,1)}), bf16[4,128,2048]{2,1,0:T(8,128)(2,1)}, u32[]{:S(2)}, u32[]{:S(2)}) async-start(bf16[4,128,2048]{2,1,0:T(8,128)(2,1)} %bitcast.16), calls=%async_computation | async-start | bytes 4194304 | tf_op jit(solution)/shard_map/all_to_all | solution.py:43
  50.3 0.0 all-gather.2.cloned.1.call-start
  50.4 0.7 all-gather.2.cloned.1.call-update
  51.1 0.0 reduce-scatter.2.cloned.1.call-start
  51.1 59.7 %all-to-all-done = bf16[4,128,2048]{2,1,0:T(8,128)(2,1)} async-done(((bf16[4,128,2048]{2,1,0:T(8,128)(2,1)}), bf16[4,128,2048]{2,1,0:T(8,128)(2,1)}, u32[]{:S(2)}, u32[]{:S(2)}) %all-to-all-start) | async-done | bytes 2097184 | tf_op jit(solution)/shard_map/all_to_all | solution.py:43
  110.8 2.1 convert_bitcast_fusion
  112.9 0.0 copy-start.2
  112.9 0.0 copy-start.5
  112.9 0.5 copy.10
  113.4 0.0 copy-start.1
  113.4 1.9 copy-done.1
  115.4 0.0 copy-done.2
  115.4 0.0 copy-done.5
  115.4 1.2 fusion
  116.6 0.0 copy-start.4
  116.6 2.2 fusion.10
  118.7 0.0 reduce-scatter.2.cloned.1.call-update
  118.8 0.0 all-reduce.6.cloned.1.call-start
  118.8 0.0 all-gather.2.cloned.1.call-done
  118.8 0.0 copy-done.4
  118.9 3.5 %convolution_multiply_fusion = f32[64,768]{1,0:T(8,128)} fusion(bf16[128,768]{1,0:T(8,128)(2,1)S(1)} %copy-done.4, bf16[8192,64]{0,1:T(8,128)(2,1)} %all-gather.2.cloned.1.call-done, bf16[128,8192]{1,0:T(8,128)(2,1)} %param.6, f32[8192]{0:T(1024)S(1)} %copy-done.5, f32[128]{0:T(128)S(1)} %get-tuple-element.7), kind=kOutput, calls=%fused_computation.13 | convolution fusion | flops 151052288 | bytes 3572224 | tf_op jit(solution)/shard_map/dot_general | solution.py:20
  122.4 39.5 %reduce-scatter.2.cloned.1.call-done = f32[2048,64]{0,1:T(8,128)} async-done(((f32[8192,64]{0,1:T(8,128)}), f32[2048,64]{0,1:T(8,128)}) %reduce-scatter.2.cloned.1.call-update) | async-done | bytes 524304 | tf_op jit(solution)/shard_map/reduce_scatter | solution.py:58
  161.9 0.0 all-reduce.6.cloned.1.call-update
  161.9 0.0 all-reduce.4.cloned.1.call-start
  161.9 36.9 %all-reduce.6.cloned.1.call-done = (f32[2048,64]{0,1:T(8,128)}, f32[64,768]{1,0:T(8,128)}) async-done(((f32[2048,64]{0,1:T(8,128)}, f32[64,768]{1,0:T(8,128)}), (f32[2048,64]{0,1:T(8,128)}, f32[64,768]{1,0:T(8,128)})) %all-reduce.6.cloned.1.call-update) | async-done | bytes 720912 | tf_op jit(solution)/shard_map/psum | solution.py:62
  198.8 1.8 multiply_reduce_fusion
  200.6 0.0 all-reduce.4.cloned.1.call-update
  200.6 5.3 %fusion.3 = bf16[128,8192]{1,0:T(8,128)(2,1)} fusion(bf16[128,8192]{1,0:T(8,128)(2,1)} %param.6, f32[128,8192]{1,0:T(8,128)} %bitcast.15, f32[128]{0:T(128)S(1)} %get-tuple-element.4, f32[128]{0:T(128)S(1)} %get-tuple-element.8, f32[8192]{0:T(1024)S(1)} %copy-done.5, f32[128]{0:T(128)S(1)} %get-tuple-element.7), kind=kLoop, calls=%fused_computation.7 | loop fusion | flops 7340032 | bytes 8422912 | tf_op jit(solution)/shard_map/convert_element_type | solution.py:66
  206.0 12.4 %psum.29 = f32[]{:T(128)} all-reduce(f32[]{:T(128)} %multiply_reduce_fusion), channel_id=1, replica_groups=mesh['groups'=2,'fsdp'=4,'dp'=2,'pair'=2] {'fsdp'}, use_global_device_ids=true, to_apply=%region_5.0 | all-reduce | flops 1 | bytes 8 | tf_op jit(solution)/shard_map/psum | solution.py:64
  218.3 17.6 %all-reduce.4.cloned.1.call-done = f32[64,768]{1,0:T(8,128)} async-done(((f32[64,768]{1,0:T(8,128)}), f32[64,768]{1,0:T(8,128)}) %all-reduce.4.cloned.1.call-update) | async-done | bytes 196624 | tf_op jit(solution)/shard_map/psum | solution.py:63
  236.0 1.6 multiply_reduce_fusion.1
  238.9 1.9 broadcast_multiply_fusion
  240.8 1.6 broadcast_multiply_fusion.1
  (1 shorter events, 0.0 us)
Async XLA Ops:
  7.2 34.8 %copy-start = (bf16[2048,768]{1,0:T(8,128)(2,1)S(1)}, bf16[2048,768]{1,0:T(8,128)(2,1)}, u32[]{:S(2)}) copy-start(bf16[2048,768]{1,0:T(8,128)(2,1)} %param.8) | copy-start | bytes 9437188
  42.0 1.8 copy-start.3
  45.9 64.9 %all-to-all-start = ((bf16[4,128,2048]{2,1,0:T(8,128)(2,1)}), bf16[4,128,2048]{2,1,0:T(8,128)(2,1)}, u32[]{:S(2)}, u32[]{:S(2)}) async-start(bf16[4,128,2048]{2,1,0:T(8,128)(2,1)} %bitcast.16), calls=%async_computation | async-start | bytes 4194304 | tf_op jit(solution)/shard_map/all_to_all | solution.py:43
  50.3 68.5 %all-gather.2.cloned.1.call-start = ((), (), s32[]{:S(2)}) async-start(), calls=%async_computation.3 | async-start | bytes 1310720 | tf_op jit(solution)/shard_map/all_gather | solution.py:49
  51.1 110.8 %reduce-scatter.2.cloned.1.call-start = ((), (), s32[]{:S(2)}) async-start(), calls=%async_computation.2 | async-start | bytes 2621440 | tf_op jit(solution)/shard_map/reduce_scatter | solution.py:58
  112.9 2.5 copy-start.2
  112.9 2.5 copy-start.5
  113.4 1.9 copy-start.1
  116.6 2.3 copy-start.4
  118.8 80.1 %all-reduce.6.cloned.1.call-start = ((), (), s32[]{:S(2)}) async-start(), calls=%async_computation.5 | async-start | bytes 1441792 | tf_op jit(solution)/shard_map/psum | solution.py:62
  161.9 74.1 %all-reduce.4.cloned.1.call-start = ((), (), s32[]{:S(2)}) async-start(), calls=%async_computation.4 | async-start | bytes 393216 | tf_op jit(solution)/shard_map/psum | solution.py:63
Sparse Core Ops, SparseCore 0:
  52.8 49.7 all-gather.1
  118.9 42.9 reduce-scatter.1
  165.1 33.6 all-reduce.5
  201.1 34.8 all-reduce.3
